TPU v7x, 256 devices: a whole 4x4x8 slice. The times are simulated.
256 devices in a mesh: panel: 2 (over z_hi), lat: 8 (over y, core), lon: 16 (over x, z_lo).
Axes of the slice: x: 4, y: 4, z: 8 (z_hi: 2, z_lo: 4; z = z_hi * 4 + z_lo), core: 2. Of those that a mesh axis runs over, the one named last changes fastest.
Arguments:
- tracers: float32 [2, 2, 36, 512, 2048], P('panel', None, None, 'lat', 'lon'), may hold values from -6 to 6
- winds: float32 [2, 2, 36, 512, 2048], P('panel', None, None, 'lat', 'lon'), may hold values from -0.3 to 0.3
- mixing: float32 [2, 35, 512, 2048], P('panel', None, 'lat', 'lon'), may hold values from 0.05 to 5
- strip_source: int32 [2, 320], replicated, may hold values from 0 to 127, as said below
- strip_tile: int32 [2, 320], replicated, may hold values from 0 to 127
- weights: bfloat16 [2, 320, 32, 64], replicated, may hold values from -1.5 to 1.5
Outputs:
- tracers_out: float32 [2, 2, 36, 512, 2048], P('panel', None, None, 'lat', 'lon')
Inputs may be any that keep to these rules, and one draw needn't show every extreme that they name: strip_source numbers a device of the other panel as its row of devices times (16) plus its column of devices. Strips 2m and 2m + 1 of a list have the same source device and lie on the same device; the pairs of strips that lie on one device come from distinct source devices. Over one panel's list, no device is named by more than 2 pairs of strips, and some device by exactly 2.
All inputs are finite; a program needn't handle non-finite values.
Results may differ from a plain program's by a relative error of at most 0.0003.
Values sent between devices are 32-bit elements; how exact they have to be, the bound alone decides.
A program may use at most 128 MiB of HBM per device.

v0:
```python
import functools

import jax
import jax.numpy as jnp
from jax import lax
from jax.experimental import pallas as pl
from jax.experimental.pallas import tpu as pltpu
from jax.sharding import PartitionSpec as P

MESH = pl.DeviceIdType.MESH
STEPS = 2
MIDS = 9
FIELDS = 72
LEVELS = 36
ROWS = 64
COLS = 128
SHARE = FIELDS // MIDS
PAD = 8
TALL = ROWS + 2 * PAD
CHUNK = 16
EAST, WEST, SOUTH, NORTH = range(4)


def mid_place(k):
    j = k // 2
    return 1 + 5 * (k % 2), 4 * (j // 2) + 1 + j % 2 - 9 * (j // 8)


def kernel(lat_n, lon_n, ssrc, stile, vsrc, tr_hbm, wd_hbm, mix_hbm, wt_hbm,
           out_hbm, sides_out, bands_out,
           sa, sb, w0, w1, mx, cf, rt, iv, wts, bd, pk, pkr, pt, ptr, hb, rw, rwr, prev,
           pay, inb0, inb1, hs, ob, rb, rs, dense, flip,
           lsem, ssem, rsem, psem, p1s, p1r, p2s, p2bs, p2r, p2br):
    panel = lax.axis_index("panel")
    lat = lax.axis_index("lat")
    lon = lax.axis_index("lon")
    me = lat * lon_n + lon
    other = 1 - panel
    has = {
        EAST: lon < lon_n - 1,
        WEST: lon > 0,
        SOUTH: lat < lat_n - 1,
        NORTH: lat > 0,
    }
    beside = {
        EAST: (panel, lat, lon + 1),
        WEST: (panel, lat, lon - 1),
        SOUTH: (panel, lat + 1, lon),
        NORTH: (panel, lat - 1, lon),
    }
    is_band = (lat == 0) | (lat == lat_n - 1)
    is_side = (lon == 0) | (lon == lon_n - 1)
    mid_id = jnp.int32(-1)
    for k in range(MIDS):
        mlat, mlon = mid_place(k)
        mid_id = jnp.where((lat == mlat) & (lon == mlon), jnp.int32(k), mid_id)
    is_mid = mid_id >= 0
    inb = (inb0, inb1)
    lane8 = lax.broadcasted_iota(jnp.int32, (8, COLS), 1)
    lane_c = lax.broadcasted_iota(jnp.int32, (CHUNK, COLS), 1)

    early = 64
    loads = [
        pltpu.make_async_copy(wd_hbm.at[0], w0, lsem.at[0]),
        pltpu.make_async_copy(
            tr_hbm.at[pl.ds(early, FIELDS - early)],
            sa.at[pl.ds(early, FIELDS - early), pl.ds(PAD, ROWS), :], lsem.at[1]),
        pltpu.make_async_copy(
            tr_hbm.at[pl.ds(0, early)], sa.at[pl.ds(0, early), pl.ds(PAD, ROWS), :], lsem.at[2]),
        pltpu.make_async_copy(wd_hbm.at[1], w1.at[:, pl.ds(PAD, ROWS), :], lsem.at[3]),
        pltpu.make_async_copy(mix_hbm, mx.at[pl.ds(1, LEVELS - 1)], lsem.at[4]),
        pltpu.make_async_copy(wt_hbm.at[other], wts, lsem.at[5]),
    ]
    for load in loads[:4]:
        load.start()

    barrier = pltpu.get_barrier_semaphore()
    for way in range(4):
        @pl.when(has[way])
        def _():
            pl.semaphore_signal(barrier, inc=1, device_id=beside[way], device_id_type=MESH)

    @pl.when(is_mid)
    def _():
        def greet(i, carry):
            pl.semaphore_signal(
                barrier, inc=1, device_id=(other, i // lon_n, i % lon_n), device_id_type=MESH)
            return carry
        lax.fori_loop(0, lat_n * lon_n, greet, 0)

    def greet_mids():
        def greet(k, carry):
            mlat, mlon = mid_place(k)
            pl.semaphore_signal(
                barrier, inc=1, device_id=(panel, mlat, mlon), device_id_type=MESH)
            return carry
        lax.fori_loop(0, MIDS, greet, 0)

    pl.when(is_band)(greet_mids)
    pl.when(is_side)(greet_mids)
    one = jnp.int32(1)
    none = jnp.int32(0)
    expect = jnp.int32(MIDS)
    for way in range(4):
        expect = expect + jnp.where(has[way], one, none)
    expect = expect + jnp.where(is_mid, jnp.int32(2 * lon_n + 2 * lat_n), none)

    zero = jnp.zeros((ROWS, COLS), jnp.float32)
    mx[0] = zero
    mx[LEVELS] = zero
    rt[0] = zero
    for step in range(STEPS):
        for way in range(2):
            @pl.when(jnp.logical_not(has[way ^ 1]))
            def _():
                pkr[step, way] = jnp.zeros((4, ROWS, COLS), jnp.float32)

            @pl.when(jnp.logical_not(has[2 + (way ^ 1)]))
            def _():
                rwr[step, way] = jnp.zeros((FIELDS + LEVELS, 2, COLS), jnp.float32)
    for way in range(2):
        @pl.when(jnp.logical_not(has[way ^ 1]))
        def _():
            ptr[way] = jnp.zeros((3, 8, COLS), jnp.float32)

    loads[0].wait()
    loads[1].wait()
    loads[4].start()
    loads[5].start()

    def fields_of(step):
        return FIELDS + LEVELS if step == 0 else FIELDS

    def groups_of(step):
        return (fields_of(step) + 31) // 32

    def rows_copy(step, way):
        part = pl.ds(0, fields_of(step))
        return pltpu.make_async_remote_copy(
            src_ref=rw.at[step, way - 2, part], dst_ref=rwr.at[step, way - 2, part],
            send_sem=ssem.at[step, way, 0], recv_sem=rsem.at[step, way, 0],
            device_id=beside[way], device_id_type=MESH)

    def columns_copy(step, way, group):
        return pltpu.make_async_remote_copy(
            src_ref=pk.at[step, group], dst_ref=pkr.at[step, way, group],
            send_sem=ssem.at[step, way, group], recv_sem=rsem.at[step, way, group],
            device_id=beside[way], device_id_type=MESH)

    def send_columns(step, group):
        for way in (EAST, WEST):
            @pl.when(has[way])
            def _():
                columns_copy(step, way, group).start()

    def packed(step, state, group, g):
        rows = pl.ds(pl.multiple_of(PAD + g * 8, 8), 8)
        bare = pl.ds(pl.multiple_of(g * 8, 8), 8)
        total = jnp.zeros((8, COLS), jnp.float32)
        for slot in range(min(32, fields_of(step) - 32 * group)):
            f = 32 * group + slot
            value = state[f, rows, :] if f < FIELDS else w0[f - FIELDS, bare, :]
            moved = pltpu.roll(value, (4 * slot + 2) % COLS, 1)
            total = jnp.where(lane8 // 4 == slot, moved, total)
        return total

    def unpacked(step, group, g, from_west, from_east):
        both = jnp.where(lane8 % 4 < 2, from_west, from_east)
        rows = pl.ds(pl.multiple_of(g * 8, 8), 8)
        for slot in range(min(32, fields_of(step) - 32 * group)):
            hb[32 * group + slot, rows, :] = pltpu.roll(both, (2 * COLS - 2 - 4 * slot) % COLS, 1)

    def pack_columns(step, state, group):
        def pack(g, carry):
            pk[step, group, pl.ds(pl.multiple_of(g * 8, 8), 8), :] = packed(step, state, group, g)
            return carry
        lax.fori_loop(0, ROWS // 8, pack, 0, unroll=2)

    def give_rows(step, state):
        def rows_of(f, carry):
            rw[step, 0, f] = state[f, PAD + ROWS - 2:PAD + ROWS, :]
            rw[step, 1, f] = state[f, PAD:PAD + 2, :]
            return carry
        lax.fori_loop(0, FIELDS, rows_of, 0, unroll=8)
        if step == 0:
            def winds_of(l, carry):
                rw[step, 0, FIELDS + l] = w1[l, PAD + ROWS - 2:PAD + ROWS, :]
                rw[step, 1, FIELDS + l] = w1[l, PAD:PAD + 2, :]
                return carry
            lax.fori_loop(0, LEVELS, winds_of, 0, unroll=4)
        for way in (SOUTH, NORTH):
            @pl.when(has[way])
            def _():
                rows_copy(step, way).start()

    def give_first_halo(state):
        pack_columns(0, state, 2)
        pl.semaphore_wait(barrier, expect)
        send_columns(0, 2)
        pack_columns(0, state, 3)
        send_columns(0, 3)
        loads[2].wait()
        loads[3].wait()
        give_rows(0, state)
        for group in range(2):
            pack_columns(0, state, group)
            send_columns(0, group)

    def take_rows(step, state):
        for way, came in ((SOUTH, NORTH), (NORTH, SOUTH)):
            @pl.when(has[came])
            def _():
                rows_copy(step, way).wait_recv()

        def rows_of(f, carry):
            state[f, PAD - 2:PAD, :] = rwr[step, 0, f]
            state[f, PAD + ROWS:PAD + ROWS + 2, :] = rwr[step, 1, f]
            return carry
        lax.fori_loop(0, FIELDS, rows_of, 0, unroll=8)
        if step == 0:
            def winds_of(l, carry):
                w1[l, PAD - 2:PAD, :] = rwr[step, 0, FIELDS + l]
                w1[l, PAD + ROWS:PAD + ROWS + 2, :] = rwr[step, 1, FIELDS + l]
                return carry
            lax.fori_loop(0, LEVELS, winds_of, 0, unroll=4)
    def take_columns(step, groups):
        for group in groups:
            for way, came in ((EAST, WEST), (WEST, EAST)):
                @pl.when(has[came])
                def _():
                    columns_copy(step, way, group).wait_recv()

            def unpack(g, carry):
                rows = pl.ds(pl.multiple_of(g * 8, 8), 8)
                unpacked(step, group, g, pkr[step, EAST, group, rows, :], pkr[step, WEST, group, rows, :])
                return carry
            lax.fori_loop(0, ROWS // 8, unpack, 0, unroll=2)

    def patch_copy(way):
        return pltpu.make_async_remote_copy(
            src_ref=pt, dst_ref=ptr.at[way], send_sem=psem.at[0, way], recv_sem=psem.at[1, way],
            device_id=beside[way], device_id_type=MESH)

    def patch_columns(step, state):
        for edge, g in ((0, 0), (lat_n - 1, ROWS // 8 - 1)):
            @pl.when(lat == edge)
            def _():
                for group in range(3):
                    pt[group] = packed(step, state, group, g)
        for way in (EAST, WEST):
            @pl.when(has[way])
            def _():
                patch_copy(way).start()

    def take_patch(step):
        for way in (EAST, WEST):
            @pl.when(has[way ^ 1])
            def _():
                patch_copy(way).wait_recv()
        for edge, g in ((0, 0), (lat_n - 1, ROWS // 8 - 1)):
            @pl.when(lat == edge)
            def _():
                for group in range(3):
                    unpacked(step, group, g, ptr[EAST, group], ptr[WEST, group])

    def sent_halo(step):
        for way in range(4):
            @pl.when(has[way])
            def _():
                if way in (EAST, WEST):
                    for group in range(groups_of(step)):
                        columns_copy(step, way, group).wait_send()
                    if step > 0:
                        pl.when(is_band)(patch_copy(way).wait_send)
                else:
                    rows_copy(step, way).wait_send()

    def pivots(l, carry):
        for g in range(ROWS // CHUNK):
            rows = pl.ds(g * CHUNK, CHUNK)
            low = mx[l, rows, :]
            high = mx[l + 1, rows, :]
            inv = 1.0 / (1.0 + low + high - low * rt[l, rows, :])
            iv[l, rows, :] = inv
            rt[l + 1, rows, :] = high * inv
            cf[l, 9, rows, :] = low * inv
        return carry

    def coefficients(l, carry):
        for g in range(ROWS // CHUNK):
            rows = pl.ds(g * CHUNK, CHUNK)
            w = w0[l, rows, :]
            beyond = hb[FIELDS + l, rows, :]
            w_east = pltpu.roll(jnp.where(lane_c < 1, beyond, w), COLS - 1, 1)
            w_west = pltpu.roll(jnp.where(lane_c >= COLS - 1, beyond, w), 1, 1)
            base = PAD + g * CHUNK
            v = w1[l, base:base + CHUNK, :]
            v_next = w1[l, base + 1:base + CHUNK + 1, :]
            v_prev = w1[l, base - 1:base + CHUNK - 1, :]

            def parts(face):
                face = face * (1.0 / 12.0)
                return jnp.maximum(face, 0.0), jnp.minimum(face, 0.0)

            pe, me_ = parts(w + w_east)
            pw, mw = parts(w + w_west)
            pn, mn = parts(v + v_next)
            ps, ms = parts(v + v_prev)
            inv = iv[l, rows, :]
            centre = 1.0 + (2.0 * (pw - me_) + 5.0 * (mw - pe)) + (2.0 * (ps - mn) + 5.0 * (ms - pn))
            for i, c in enumerate((
                centre,
                -pw, 5.0 * pw + 2.0 * mw + pe, -mw - 2.0 * pe - 5.0 * me_, me_,
                -ps, 5.0 * ps + 2.0 * ms + pn, -ms - 2.0 * pn - 5.0 * mn, mn,
            )):
                cf[l, i, rows, :] = c * inv
        return carry

    def forward(state, new, chunks):
        for g in chunks:
            prev[:, g * CHUNK:g * CHUNK + CHUNK, :] = jnp.zeros((2, CHUNK, COLS), jnp.float32)

        def level(l, carry):
            for g in chunks:
                rows = pl.ds(g * CHUNK, CHUNK)
                base = PAD + g * CHUNK
                for t in range(2):
                    f = t * LEVELS + l
                    q = state[f, base:base + CHUNK, :]
                    beyond = hb[f, rows, :]
                    x = cf[l, 0, rows, :] * q
                    x += cf[l, 1, rows, :] * pltpu.roll(jnp.where(lane_c >= COLS - 2, beyond, q), 2, 1)
                    x += cf[l, 2, rows, :] * pltpu.roll(jnp.where(lane_c >= COLS - 1, beyond, q), 1, 1)
                    x += cf[l, 3, rows, :] * pltpu.roll(jnp.where(lane_c < 1, beyond, q), COLS - 1, 1)
                    x += cf[l, 4, rows, :] * pltpu.roll(jnp.where(lane_c < 2, beyond, q), COLS - 2, 1)
                    x += cf[l, 5, rows, :] * state[f, base - 2:base - 2 + CHUNK, :]
                    x += cf[l, 6, rows, :] * state[f, base - 1:base - 1 + CHUNK, :]
                    x += cf[l, 7, rows, :] * state[f, base + 1:base + 1 + CHUNK, :]
                    x += cf[l, 8, rows, :] * state[f, base + 2:base + 2 + CHUNK, :]
                    x += cf[l, 9, rows, :] * prev[t, rows, :]
                    prev[t, rows, :] = x
                    new[f, base:base + CHUNK, :] = x
            return carry
        lax.fori_loop(0, LEVELS, level, 0, unroll=8 // len(chunks))

    def backward(new, chunks):
        def level(i, carry):
            l = LEVELS - 2 - i
            for g in chunks:
                rows = pl.ds(g * CHUNK, CHUNK)
                base = PAD + g * CHUNK
                for t in range(2):
                    f = t * LEVELS + l
                    x = new[f, base:base + CHUNK, :] + rt[l + 1, rows, :] * prev[t, rows, :]
                    prev[t, rows, :] = x
                    new[f, base:base + CHUNK, :] = x
            return carry
        lax.fori_loop(0, LEVELS - 1, level, 0, unroll=5)

    def to_mid(step, k):
        mlat, mlon = mid_place(k)
        return pltpu.make_async_remote_copy(
            src_ref=pay.at[step, k], dst_ref=inb[step].at[me], send_sem=p1s.at[step],
            recv_sem=p1r.at[step], device_id=(other, mlat, mlon), device_id_type=MESH)

    def to_band(step, d):
        return pltpu.make_async_remote_copy(
            src_ref=ob.at[step, pl.ds(2 * d, 2)], dst_ref=rb.at[step, mid_id],
            send_sem=p2bs.at[step], recv_sem=p2br.at[step],
            device_id=(panel, (d // lon_n) * (lat_n - 1), d % lon_n), device_id_type=MESH)

    def to_side(step, e):
        return pltpu.make_async_remote_copy(
            src_ref=ob.at[step, 4 * lon_n + e], dst_ref=rs.at[step, mid_id],
            send_sem=p2s.at[step], recv_sem=p2r.at[step],
            device_id=(panel, e % lat_n, (e // lat_n) * (lon_n - 1)), device_id_type=MESH)

    def all_of(ref, sem):
        pltpu.make_async_copy(ref, ref, sem).wait()

    def provide(step, new, tiles):
        flat = new.reshape(FIELDS * TALL, COLS)
        lane_f = lax.broadcasted_iota(jnp.int32, (FIELDS, COLS), 1)
        total = jnp.zeros((FIELDS, COLS), jnp.float32)
        for pair in range(2):
            cells = jnp.zeros((FIELDS, COLS), jnp.float32)
            for s in range(2):
                tile = tiles[2 * pair + s]
                first = PAD + (tile // 8) * 4
                for r in range(4):
                    row = flat[pl.ds(first + r, FIELDS, stride=TALL), :]
                    shift = (2 * COLS + 64 * s + 16 * r - 16 * (tile % 8)) % COLS
                    row = pltpu.roll(row, shift, 1)
                    cells = jnp.where(lane_f // 16 == 4 * s + r, row, cells)
            w = bd[128 * pair:128 * pair + 128, :]
            rest = cells
            for part in range(3):
                piece = rest.astype(jnp.bfloat16)
                total += jnp.dot(piece, w, preferred_element_type=jnp.float32)
                if part < 2:
                    rest = rest - piece.astype(jnp.float32)
        pay[step] = total.reshape(MIDS, SHARE, COLS)

    def route(step):
        def send(k, carry):
            to_mid(step, k).start()
            return carry
        lax.fori_loop(0, MIDS, send, 0)

    def sort_and_send(step):
        @pl.when(is_mid)
        def _():
            if step == 0:
                pairs = ssrc.shape[1] // 2
                shape = (pairs, 2 * pairs)
                row = jnp.where(panel == 0, vsrc[0:1, :], vsrc[1:2, :]).astype(jnp.float32)
                row = jnp.broadcast_to(row, shape)
                lane = lax.broadcasted_iota(jnp.int32, shape, 1)
                pair = lax.broadcasted_iota(jnp.int32, shape, 0)
                own = jnp.sum(jnp.where(lane == 2 * pair, row, 0.0), axis=1, keepdims=True)
                same = (row == own) & (lane % 2 == 0) & (lane < 2 * pair)
                second = jnp.max(jnp.where(same, 1.0, 0.0), axis=1, keepdims=True)
                hs[...] = jnp.broadcast_to(second, (pairs, COLS)).reshape(pairs // 8, 8, COLS)
            all_of(inb[step], p1r.at[step])
            lane_s = lax.broadcasted_iota(jnp.int32, (SHARE, COLS), 1)
            batch = 8

            def sort(i):
                done = []
                for j in range(batch):
                    u = i * batch + j
                    a = inb[step][ssrc[panel, 4 * u]]
                    b = inb[step][ssrc[panel, 4 * u + 2]]
                    line = hs[2 * i + j // 4]
                    second_a = line[2 * j % 8:2 * j % 8 + 1, :] > 0.5
                    second_b = line[2 * j % 8 + 1:2 * j % 8 + 2, :] > 0.5
                    a = jnp.where(second_a, pltpu.roll(a, 64, 1), a)
                    b = jnp.where(second_b, b, pltpu.roll(b, 64, 1))
                    done.append(jnp.where(lane_s < 64, a, b))
                for j in range(batch):
                    ob[step, i * batch + j] = done[j]

            def sides(i, carry):
                sort(4 * lon_n // batch + i)
                for j in range(batch):
                    to_side(step, batch * i + j).start()
                return carry
            lax.fori_loop(0, 2 * lat_n // batch, sides, 0)

            def bands(i, carry):
                sort(i)
                for j in range(batch // 2):
                    to_band(step, batch // 2 * i + j).start()
                return carry
            lax.fori_loop(0, 4 * lon_n // batch, bands, 0)

    def side_lines(step):
        all_of(rs.at[step], p2r.at[step])
        dense[0, 0:FIELDS, :] = rs[step].reshape(FIELDS, COLS)
        flip[...] = jnp.transpose(dense[0])
        first = flip[pl.ds(0, ROWS, stride=2), :]
        second = pltpu.roll(flip[pl.ds(1, ROWS, stride=2), :], 1, 1)
        even = lax.broadcasted_iota(jnp.int32, (ROWS, COLS), 1) % 2 == 0
        start = jnp.where(lon == 0, 0, COLS - 2)
        return (pltpu.roll(jnp.where(even, first, second), start, 1),
                pltpu.roll(jnp.where(even, second, first), start, 1))

    def band_lines(step):
        all_of(rb.at[step], p2br.at[step])
        lane_f = lax.broadcasted_iota(jnp.int32, (FIELDS, COLS), 1)
        lines = []
        for r in range(2):
            line = jnp.zeros((FIELDS, COLS), jnp.float32)
            for u in range(2):
                tiles = rb[step, :, u].reshape(FIELDS, COLS)
                for s in range(4):
                    moved = pltpu.roll(tiles, (2 * COLS + 64 * u - 16 * s - 16 * r) % COLS, 1)
                    line = jnp.where(lane_f // 16 == 4 * u + s, moved, line)
            lines.append(line)
        return lines

    def fill(step, new):
        @pl.when(is_side)
        def _():
            dense[0, 0:ROWS, :], dense[1, 0:ROWS, :] = side_lines(step)
            start = jnp.where(lon == 0, 0, COLS - 2)

            def column(g, carry):
                rows = pl.ds(pl.multiple_of(PAD + g * 8, 8), 8)
                bare = pl.ds(pl.multiple_of(g * 8, 8), 8)
                pair = dense[0, bare, :], dense[1, bare, :]
                for f in range(FIELDS):
                    a = pltpu.roll(pair[f % 2], COLS - f, 1) if f else pair[0]
                    new[f, rows, :] = jnp.where(lane8 // 2 == start // 2, a, new[f, rows, :])
                return carry
            lax.fori_loop(0, ROWS // 8, column, 0)

        @pl.when(is_band)
        def _():
            lines = band_lines(step)
            flat = new.reshape(FIELDS * TALL, COLS)
            for r in range(2):
                @pl.when(lat == 0)
                def _():
                    flat[pl.ds(PAD + r, FIELDS, stride=TALL), :] = lines[r]

                @pl.when(lat == lat_n - 1)
                def _():
                    flat[pl.ds(PAD + ROWS - 2 + r, FIELDS, stride=TALL), :] = lines[r]

    def hand_on(step):
        @pl.when(is_side)
        def _():
            sides_out[0], sides_out[1] = side_lines(step)

        @pl.when(is_band)
        def _():
            bands_out[0], bands_out[1] = band_lines(step)

    def pick_weights(strips):
        entries = wts.shape[1]
        lane = lax.broadcasted_iota(jnp.int32, (entries, COLS), 1)
        wanted = jnp.zeros((entries, COLS), jnp.int32)
        for b in range(4):
            wanted = jnp.where(lane // 32 == b, strips[b], wanted)
        entry = lax.broadcasted_iota(jnp.int32, (entries, COLS), 0)
        one_hot = jnp.where(entry == wanted, 1.0, 0.0).astype(jnp.bfloat16)
        lane_k = lax.broadcasted_iota(jnp.int32, (64, COLS), 1)

        def cell(c, total):
            rows = wts[pl.ds(pl.multiple_of(c * 64, 64), 64), :]
            mine = jnp.dot(rows, one_hot, preferred_element_type=jnp.float32)
            return jnp.where(lane_k % 32 == c, mine, total)
        total = lax.fori_loop(0, 32, cell, jnp.zeros((64, COLS), jnp.float32), unroll=4)
        for b in range(4):
            bd[64 * b:64 * b + 64, :] = jnp.where(lane_k // 32 == b, total, 0.0).astype(jnp.bfloat16)

    give_first_halo(sa)

    def look(i, found):
        first, second = found
        for j in range(8):
            m = 8 * i + j
            hit = ssrc[other, 2 * m] == me
            second = jnp.where(hit & (first >= 0), m, second)
            first = jnp.where(hit & (first < 0), m, first)
        return first, second
    found = lax.fori_loop(0, ssrc.shape[1] // 16, look, (jnp.int32(-1), jnp.int32(-1)))
    found = [jnp.maximum(m, 0) for m in found]
    strips = [2 * m + s for m in found for s in range(2)]
    tiles = [stile[other, strip] for strip in strips]

    loads[4].wait()
    lax.fori_loop(0, LEVELS, pivots, 0, unroll=2)
    loads[5].wait()
    pick_weights(strips)
    take_rows(0, sa)
    take_columns(0, (2, 3))
    lax.fori_loop(0, LEVELS, coefficients, 0, unroll=2)
    take_columns(0, (0, 1))
    for step in range(STEPS):
        state, new = (sa, sb) if step % 2 == 0 else (sb, sa)
        if step == 0:
            inner, outer = (), tuple(range(ROWS // CHUNK))
        else:
            inner, outer = tuple(range(1, ROWS // CHUNK - 1)), (0, ROWS // CHUNK - 1)
            forward(state, new, inner)
            backward(new, inner)
            pl.when(is_band)(lambda: take_patch(step))

            @pl.when(is_side)
            def _():
                take_rows(step, state)
        forward(state, new, outer)
        backward(new, outer)
        if step == STEPS - 1:
            store = pltpu.make_async_copy(new.at[:, pl.ds(PAD, ROWS), :], out_hbm, lsem.at[0])
            store.start()
        provide(step, new, tiles)
        route(step)
        if step == STEPS - 1:
            sort_and_send(step)
            hand_on(step)
        else:
            later = step + 1
            for group in range(3):
                pack_columns(later, new, group)
                send_columns(later, group)
            pl.when(jnp.logical_not(is_side))(lambda: give_rows(later, new))
            sort_and_send(step)
            take_columns(later, (0, 1, 2))
            pl.when(jnp.logical_not(is_side))(lambda: take_rows(later, new))
            fill(step, new)

            @pl.when(is_side)
            def _():
                give_rows(later, new)
            pl.when(is_band)(lambda: patch_columns(later, new))

    for step in range(STEPS):
        sent_halo(step)
        all_of(pay.at[step], p1s.at[step])

        @pl.when(is_mid)
        def _():
            all_of(ob.at[step, pl.ds(0, 4 * lon_n)], p2bs.at[step])
            all_of(ob.at[step, pl.ds(4 * lon_n, 2 * lat_n)], p2s.at[step])
    store.wait()


def last_fill(lat_n, lon_n, chunks, state, sides, bands, out, held, side, band, rsem, wsem, lsem):
    lat = lax.axis_index("lat")
    lon = lax.axis_index("lon")
    count = FIELDS // chunks
    is_side = (lon == 0) | (lon == lon_n - 1)
    is_band = (lat == 0) | (lat == lat_n - 1)
    start = jnp.where(lon == 0, 0, COLS - 2)
    lane = lax.broadcasted_iota(jnp.int32, (ROWS, COLS), 1)
    get_side = pltpu.make_async_copy(sides, side, lsem.at[0])
    get_band = pltpu.make_async_copy(bands, band, lsem.at[1])
    pl.when(is_side)(get_side.start)
    pl.when(is_band)(get_band.start)
    parts = [pl.ds(c * count, count) for c in range(chunks)]
    reads = [pltpu.make_async_copy(state.at[p], held.at[p], rsem.at[c]) for c, p in enumerate(parts)]
    writes = [pltpu.make_async_copy(held.at[p], out.at[p], wsem.at[c]) for c, p in enumerate(parts)]
    for read in reads:
        read.start()
    pl.when(is_side)(get_side.wait)
    pl.when(is_band)(get_band.wait)
    for c in range(chunks):
        reads[c].wait()
        fields = range(c * count, c * count + count)

        @pl.when(is_side)
        def _():
            for f in fields:
                a = pltpu.roll(side[f % 2], COLS - f, 1) if f else side[0]
                held[f] = jnp.where(lane // 2 == start // 2, a, held[f])

        for edge, row in ((0, 0), (lat_n - 1, ROWS - 2)):
            @pl.when(lat == edge)
            def _():
                for f in fields:
                    for r in range(2):
                        held[f, row + r:row + r + 1, :] = band[r, f:f + 1, :]

        writes[c].start()
    for write in writes:
        write.wait()


def on_device(lat_n, lon_n, tracers, winds, mixing, strip_source, strip_tile, weights):
    f32 = jnp.float32
    vm = pltpu.VMEM
    dma = pltpu.SemaphoreType.DMA
    devices = lat_n * lon_n
    tiles_out = 4 * lon_n + 2 * lat_n
    anywhere = pl.BlockSpec(memory_space=pl.ANY)
    smem = pl.BlockSpec(memory_space=pltpu.SMEM)
    in_vmem = pl.BlockSpec(memory_space=pltpu.VMEM)
    state, sides, bands = pl.pallas_call(
        functools.partial(kernel, lat_n, lon_n),
        out_shape=(
            jax.ShapeDtypeStruct((FIELDS, ROWS, COLS), f32),
            jax.ShapeDtypeStruct((2, ROWS, COLS), f32),
            jax.ShapeDtypeStruct((2, FIELDS, COLS), f32),
        ),
        in_specs=[smem, smem, in_vmem, anywhere, anywhere, anywhere, anywhere],
        out_specs=(anywhere, in_vmem, in_vmem),
        scratch_shapes=[
            vm((FIELDS, TALL, COLS), f32),
            vm((FIELDS, TALL, COLS), f32),
            vm((LEVELS, ROWS, COLS), f32),
            vm((LEVELS, TALL, COLS), f32),
            vm((LEVELS + 1, ROWS, COLS), f32),
            vm((LEVELS, 10, ROWS, COLS), f32),
            vm((LEVELS + 1, ROWS, COLS), f32),
            vm((LEVELS, ROWS, COLS), f32),
            vm((32 * 64, weights.shape[1]), weights.dtype),
            vm((256, COLS), jnp.bfloat16),
            vm((STEPS, 4, ROWS, COLS), f32),
            vm((STEPS, 2, 4, ROWS, COLS), f32),
            vm((3, 8, COLS), f32),
            vm((2, 3, 8, COLS), f32),
            vm((FIELDS + LEVELS, ROWS, COLS), f32),
            vm((STEPS, 2, FIELDS + LEVELS, 2, COLS), f32),
            vm((STEPS, 2, FIELDS + LEVELS, 2, COLS), f32),
            vm((2, ROWS, COLS), f32),
            vm((STEPS, MIDS, SHARE, COLS), f32),
            vm((devices, SHARE, COLS), f32),
            vm((devices, SHARE, COLS), f32),
            vm((strip_source.shape[1] // 16, 8, COLS), f32),
            vm((STEPS, tiles_out, SHARE, COLS), f32),
            vm((STEPS, MIDS, 2, SHARE, COLS), f32),
            vm((STEPS, MIDS, SHARE, COLS), f32),
            vm((2, 128, COLS), f32),
            vm((128, COLS), f32),
            dma((6,)),
            dma((STEPS, 4, 4)),
            dma((STEPS, 4, 4)),
            dma((2, 2)),
            dma((STEPS,)),
            dma((STEPS,)),
            dma((STEPS,)),
            dma((STEPS,)),
            dma((STEPS,)),
            dma((STEPS,)),
        ],
        compiler_params=pltpu.CompilerParams(
            collective_id=0, has_side_effects=True, vmem_limit_bytes=56 * 1024 * 1024),
    )(
        strip_source, strip_tile, strip_source,
        tracers.reshape(FIELDS, ROWS, COLS),
        winds.reshape(2, LEVELS, ROWS, COLS),
        mixing.reshape(LEVELS - 1, ROWS, COLS),
        jnp.transpose(weights, (0, 2, 3, 1)).reshape(2, 32 * 64, weights.shape[1]),
    )
    chunks = 6
    out = pl.pallas_call(
        functools.partial(last_fill, lat_n, lon_n, chunks),
        out_shape=jax.ShapeDtypeStruct((FIELDS, ROWS, COLS), f32),
        in_specs=[anywhere, anywhere, anywhere],
        out_specs=anywhere,
        scratch_shapes=[
            vm((FIELDS, ROWS, COLS), f32),
            vm((2, ROWS, COLS), f32),
            vm((2, FIELDS, COLS), f32),
            dma((chunks,)),
            dma((chunks,)),
            dma((2,)),
        ],
        compiler_params=pltpu.CompilerParams(vmem_limit_bytes=56 * 1024 * 1024),
    )(state, sides, bands)
    return out.reshape(tracers.shape)


def solution(mesh):
    return jax.shard_map(
        functools.partial(on_device, mesh.shape["lat"], mesh.shape["lon"]),
        mesh=mesh,
        in_specs=(
            P("panel", None, None, "lat", "lon"),
            P("panel", None, None, "lat", "lon"),
            P("panel", None, "lat", "lon"),
            P(),
            P(),
            P(),
        ),
        out_specs=P("panel", None, None, "lat", "lon"),
        check_vma=False,
    )
```

profile of v0, /device:TPU:1, one launch (start us, length us, event | category | flops | bytes accessed | tf_op | source)
XLA Modules:
  0.0 66.4 jit_solution(8307845571350025420)
XLA Ops:
  0.0 63.1 %shard_map.64 = (f32[72,64,128]{2,1,0:T(8,128)}, f32[2,64,128]{2,1,0:T(8,128)}, f32[2,72,128]{2,1,0:T(8,128)}) custom-call(s32[2,320]{1,0:T(2,128)} %vsrc.1, s32[2,320]{1,0:T(2,128)} %stile.1, s32[2,320]{1,0:T(2,128)} %vsrc.1, f32[72,64,128]{2,1,0:T(8,128)} %bitcast.8, f32[2,36,64,128]{3,2,1,0:T(8,128)} %bitcast.9, f32[35,64,128]{2,1,0:T(8,128)} %bitcast.10, ...), custom_call_target="tpu_custom_call" | custom-call | tf_op jit(solution)/shard_map/pallas_call | solution.py:661
  63.1 3.3 %shard_map.65 = f32[72,64,128]{2,1,0:T(8,128)} custom-call(f32[72,64,128]{2,1,0:T(8,128)} %get-tuple-element.8.state, f32[2,64,128]{2,1,0:T(8,128)} %get-tuple-element.9.sides, f32[2,72,128]{2,1,0:T(8,128)} %get-tuple-element.10.bands), custom_call_target="tpu_custom_call" | custom-call | tf_op jit(solution)/shard_map/pallas_call | solution.py:719
where the time goes:
time: 66.6 us; the launch traced here: 66.4 us
  Pallas kernels  66.4 us (100%)
    pallas_call x1, Pallas kernels, on_device(): pl.pallas_call(functools.partial(kernel, lat_n, lon_n), out_shape=(jax.Sh...  63.1 us
    pallas_call x1, Pallas kernels, on_device(): pl.pallas_call(functools.partial(last_fill, lat_n, lon_n, chunks), out_sh...  3.32 us

commit v1 on v0

--- a/solution.py
+++ b/solution.py
@@ -341,7 +341,7 @@
                     prev[t, rows, :] = x
                     new[f, base:base + CHUNK, :] = x
             return carry
-        lax.fori_loop(0, LEVELS, level, 0, unroll=8 // len(chunks))
+        lax.fori_loop(0, LEVELS, level, 0, unroll=12 // len(chunks))
 
     def backward(new, chunks):
         def level(i, carry):
@@ -431,7 +431,7 @@
                     u = i * batch + j
                     a = inb[step][ssrc[panel, 4 * u]]
                     b = inb[step][ssrc[panel, 4 * u + 2]]
-                    line = hs[2 * i + j // 4]
+                    line = hs[batch // 4 * i + j // 4]
                     second_a = line[2 * j % 8:2 * j % 8 + 1, :] > 0.5
                     second_b = line[2 * j % 8 + 1:2 * j % 8 + 2, :] > 0.5
                     a = jnp.where(second_a, pltpu.roll(a, 64, 1), a)
@@ -479,21 +479,30 @@
             lines.append(line)
         return lines
 
+    def fill_column(new, g):
+        start = jnp.where(lon == 0, 0, COLS - 2)
+        rows = pl.ds(pl.multiple_of(PAD + g * 8, 8), 8)
+        bare = pl.ds(pl.multiple_of(g * 8, 8), 8)
+        pair = dense[0, bare, :], dense[1, bare, :]
+        for f in range(FIELDS):
+            a = pltpu.roll(pair[f % 2], COLS - f, 1) if f else pair[0]
+            new[f, rows, :] = jnp.where(lane8 // 2 == start // 2, a, new[f, rows, :])
+
+    def fill_middle(new):
+        def column(g, carry):
+            fill_column(new, g)
+            return carry
+        lax.fori_loop(1, ROWS // 8 - 1, column, 0)
+
     def fill(step, new):
         @pl.when(is_side)
         def _():
             dense[0, 0:ROWS, :], dense[1, 0:ROWS, :] = side_lines(step)
-            start = jnp.where(lon == 0, 0, COLS - 2)
-
-            def column(g, carry):
-                rows = pl.ds(pl.multiple_of(PAD + g * 8, 8), 8)
-                bare = pl.ds(pl.multiple_of(g * 8, 8), 8)
-                pair = dense[0, bare, :], dense[1, bare, :]
-                for f in range(FIELDS):
-                    a = pltpu.roll(pair[f % 2], COLS - f, 1) if f else pair[0]
-                    new[f, rows, :] = jnp.where(lane8 // 2 == start // 2, a, new[f, rows, :])
+
+            def column(i, carry):
+                fill_column(new, i * (ROWS // 8 - 1))
                 return carry
-            lax.fori_loop(0, ROWS // 8, column, 0)
+            lax.fori_loop(0, 2, column, 0)
 
         @pl.when(is_band)
         def _():
@@ -556,7 +565,7 @@
     pick_weights(strips)
     take_rows(0, sa)
     take_columns(0, (2, 3))
-    lax.fori_loop(0, LEVELS, coefficients, 0, unroll=2)
+    lax.fori_loop(0, LEVELS, coefficients, 0, unroll=3)
     take_columns(0, (0, 1))
     for step in range(STEPS):
         state, new = (sa, sb) if step % 2 == 0 else (sb, sa)
@@ -596,6 +605,7 @@
             def _():
                 give_rows(later, new)
             pl.when(is_band)(lambda: patch_columns(later, new))
+            pl.when(is_side)(lambda: fill_middle(new))
 
     for step in range(STEPS):
         sent_halo(step)
@@ -715,7 +725,7 @@
         mixing.reshape(LEVELS - 1, ROWS, COLS),
         jnp.transpose(weights, (0, 2, 3, 1)).reshape(2, 32 * 64, weights.shape[1]),
     )
-    chunks = 6
+    chunks = 4
     out = pl.pallas_call(
         functools.partial(last_fill, lat_n, lon_n, chunks),
         out_shape=jax.ShapeDtypeStruct((FIELDS, ROWS, COLS), f32),

time: 66.6 us -> 65.9 us (0.989)
  Pallas kernels: 66.4 us -> 65.7 us
where the time goes in v1:
time: 65.9 us; the launch traced here: 65.7 us
  Pallas kernels  65.7 us (100%)
    pallas_call x1, Pallas kernels, on_device(): pl.pallas_call(functools.partial(kernel, lat_n, lon_n), out_shape=(jax.Sh...  62.6 us
    pallas_call x1, Pallas kernels, on_device(): pl.pallas_call(functools.partial(last_fill, lat_n, lon_n, chunks), out_sh...  3.15 us

profile of v1, /device:TPU:1, one launch (start us, length us, event | category | flops | bytes accessed | tf_op | source)
XLA Modules:
  0.0 65.7 jit_solution(14483358558674838286)
XLA Ops:
  0.0 62.6 %shard_map.64 = (f32[72,64,128]{2,1,0:T(8,128)}, f32[2,64,128]{2,1,0:T(8,128)}, f32[2,72,128]{2,1,0:T(8,128)}) custom-call(s32[2,320]{1,0:T(2,128)} %vsrc.1, s32[2,320]{1,0:T(2,128)} %stile.1, s32[2,320]{1,0:T(2,128)} %vsrc.1, f32[72,64,128]{2,1,0:T(8,128)} %bitcast.8, f32[2,36,64,128]{3,2,1,0:T(8,128)} %bitcast.9, f32[35,64,128]{2,1,0:T(8,128)} %bitcast.10, ...), custom_call_target="tpu_custom_call" | custom-call | tf_op jit(solution)/shard_map/pallas_call | solution.py:671
  62.6 3.2 %shard_map.65 = f32[72,64,128]{2,1,0:T(8,128)} custom-call(f32[72,64,128]{2,1,0:T(8,128)} %get-tuple-element.8.state, f32[2,64,128]{2,1,0:T(8,128)} %get-tuple-element.9.sides, f32[2,72,128]{2,1,0:T(8,128)} %get-tuple-element.10.bands), custom_call_target="tpu_custom_call" | custom-call | tf_op jit(solution)/shard_map/pallas_call | solution.py:729
